TPU v7x, 256 devices: a whole 4x4x8 slice. The times are simulated.
256 devices in a mesh: srow: 16 (over x, y_hi, core), scol: 16 (over z, y_lo).
Axes of the slice: x: 4, y: 4 (y_hi: 2, y_lo: 2; y = y_hi * 2 + y_lo), z: 8, core: 2. Of those that a mesh axis runs over, the one named last changes fastest.
Arguments:
- patterns: float32 [64, 64, 128, 128], P('srow', 'scol'), may hold values from 0.01 to 800, as said below
- offsets: int32 [64, 64, 2], P('srow', 'scol'), may hold values from 0 to 71, as said below
- object_field: float32 [2, 1152, 1152], P(None, 'srow', 'scol'), may hold values from -5 to 5
- probe: float32 [2, 2, 128, 128], replicated, may hold values from -6 to 6
Outputs:
- new_object: float32 [2, 1152, 1152], P(None, 'srow', 'scol')
- new_probe: float32 [2, 2, 128, 128], replicated
Inputs may be any that keep to these rules, and one draw needn't show every extreme that they name: `patterns`: patterns are positive. `offsets`: position (r, c) has its centre at tile row 16 * (r mod 4) plus 0 to 23, and tile column 16 * (c mod 4) plus 0 to 23.
All inputs are finite; a program needn't handle non-finite values.
Results may differ from a plain program's by a relative error of at most 0.0003.
Values sent between devices are 32-bit elements; how exact they have to be, the bound alone decides.
No kernel may reach another device: no remote copies, remote signals or barrier semaphores. Data moves between devices by JAX's collectives and lax.ppermute only.
A program may use at most 64 MiB of HBM per device.

v0:
```python
import math
import jax
import jax.numpy as jnp
from jax import lax
from jax.sharding import PartitionSpec as P

W = 128
PR = 4
PC = 4
obj_rate = 0.2
probe_rate = 0.5
amp_floor = 0.1
highest = lax.Precision.HIGHEST


def extended_2(cells, sides, width):
    for axis, dim in sides:
        count = lax.axis_size(axis)
        head = lax.slice_in_dim(cells, 0, width, axis=dim)
        tail = lax.slice_in_dim(cells, cells.shape[dim] - width, cells.shape[dim], axis=dim)
        cells = jnp.concatenate(
            [
                lax.ppermute(tail, axis, [(i, (i + 1) % count) for i in range(count)]),
                cells,
                lax.ppermute(head, axis, [((i + 1) % count, i) for i in range(count)]),
            ],
            axis=dim,
        )
    return cells


def signed_freq(length):
    counter = jnp.arange(length, dtype=jnp.int32)
    return ((counter + length // 2) % length - length // 2).astype(jnp.float32)


def dft_tables(length):
    counter = jnp.arange(length, dtype=jnp.int32)
    product = counter[:, None] * counter[None, :] % length
    angles = 2.0 * math.pi / length * product.astype(jnp.float32)
    return (jnp.cos(angles), jnp.sin(angles))


def rows_by(matrix, values):
    return jnp.einsum("uk,...kv->...uv", matrix, values, precision=highest)


def cols_by(values, matrix):
    return jnp.einsum("...uk,kv->...uv", values, matrix, precision=highest)


def transform(real_part, imag_part, cos_table, sin_table, turn_sign, real_only=False):
    length = cos_table.shape[0]
    if imag_part is None:
        first_re = rows_by(cos_table, real_part)
        first_im = turn_sign * rows_by(sin_table, real_part)
    else:
        first_re = rows_by(cos_table, real_part) - turn_sign * rows_by(sin_table, imag_part)
        first_im = rows_by(cos_table, imag_part) + turn_sign * rows_by(sin_table, real_part)
    second_re = (cols_by(first_re, cos_table) - turn_sign * cols_by(first_im, sin_table)) / length
    if real_only:
        return second_re
    second_im = (cols_by(first_im, cos_table) + turn_sign * cols_by(first_re, sin_table)) / length
    return (second_re, second_im)


def fold_rims(values, axis_dim, tile_len, half_width):
    full_len = values.shape[axis_dim]
    interior = lax.slice_in_dim(values, 2 * half_width, 2 * half_width + tile_len, axis=axis_dim)
    low_rim = lax.slice_in_dim(values, 0, half_width, axis=axis_dim)
    high_rim = lax.slice_in_dim(values, full_len - half_width, full_len, axis=axis_dim)
    low_pad = [
        (0, tile_len - half_width) if place == axis_dim else (0, 0) for place in range(values.ndim)
    ]
    high_pad = [
        (tile_len - half_width, 0) if place == axis_dim else (0, 0) for place in range(values.ndim)
    ]
    return interior + jnp.pad(low_rim, low_pad) + jnp.pad(high_rim, high_pad)


def on_device(patterns, offsets, object_field, probe):
    row_dev = lax.axis_size("srow")
    col_dev = lax.axis_size("scol")
    half_width = W // 2
    cos_table, sin_table = dft_tables(W)
    frequency = signed_freq(W)
    weights = jnp.sum(patterns, axis=(2, 3))
    com_row = jnp.einsum("abij,i->ab", patterns, frequency, precision=highest) / weights
    com_col = jnp.einsum("abij,j->ab", patterns, frequency, precision=highest) / weights
    centres = jnp.stack([com_row, com_col])
    row_pos = (
        (lax.axis_index("srow") * PR + jnp.arange(PR, dtype=jnp.int32)).astype(jnp.float32) + 0.5
    ) / (PR * row_dev) - 0.5
    col_pos = (
        (lax.axis_index("scol") * PC + jnp.arange(PC, dtype=jnp.int32)).astype(jnp.float32) + 0.5
    ) / (PC * col_dev) - 0.5
    row_grid = jnp.broadcast_to(row_pos[:, None], (PR, PC))
    col_grid = jnp.broadcast_to(col_pos[None, :], (PR, PC))
    first_sums = jnp.stack(
        [jnp.sum(weights), jnp.sum(weights * row_grid), jnp.sum(weights * col_grid)]
    )
    centre_moment = jnp.einsum("kab,ab->k", centres, weights, precision=highest)
    first_sums, centre_moment = lax.psum((first_sums, centre_moment), ("srow", "scol"))
    mean_row = first_sums[1] / first_sums[0]
    mean_col = first_sums[2] / first_sums[0]
    mean_centre = centre_moment / first_sums[0]
    spread = jnp.stack([row_grid - mean_row, col_grid - mean_col])
    deviation = centres - mean_centre[:, None, None]
    second_mom = jnp.einsum("iab,jab,ab->ij", spread, spread, weights, precision=highest)
    cross_mom = jnp.einsum("iab,kab,ab->ik", spread, deviation, weights, precision=highest)
    second_mom, cross_mom = lax.psum((second_mom, cross_mom), ("srow", "scol"))
    determ = second_mom[0, 0] * second_mom[1, 1] - second_mom[0, 1] * second_mom[1, 0]
    inverse = (
        jnp.stack(
            [
                jnp.stack([second_mom[1, 1], -second_mom[0, 1]]),
                jnp.stack([-second_mom[1, 0], second_mom[0, 0]]),
            ]
        )
        / determ
    )
    slopes = jnp.dot(inverse, cross_mom, precision=highest)
    descan = mean_centre[:, None, None] + jnp.einsum(
        "iab,ik->kab", spread, slopes, precision=highest
    )
    extended = extended_2(object_field, (("srow", 1), ("scol", 2)), half_width)
    pattern_flat = patterns.reshape(-1, W, W)
    spec_re, spec_im = transform(pattern_flat, None, cos_table, sin_table, -1.0)
    shift_r = descan[0].reshape(-1)
    shift_c = descan[1].reshape(-1)
    phases = (
        2.0
        * math.pi
        / W
        * (
            shift_r[:, None, None] * frequency[None, :, None]
            + shift_c[:, None, None] * frequency[None, None, :]
        )
    )
    turn_cos = jnp.cos(phases)
    turn_sin = jnp.sin(phases)
    rot_re = spec_re * turn_cos - spec_im * turn_sin
    rot_im = spec_re * turn_sin + spec_im * turn_cos
    shifted = transform(rot_re, rot_im, cos_table, sin_table, 1.0, real_only=True)
    targets = jnp.sqrt(jnp.maximum(shifted, 0.0))
    row_start = offsets[:, :, 0].reshape(-1)
    col_start = offsets[:, :, 1].reshape(-1)
    position_count = row_start.shape[0]

    def cut_one(place, gathered):
        corner = (jnp.int32(0), row_start[place], col_start[place])
        piece = lax.dynamic_slice(extended, corner, (2, W, W))
        return lax.dynamic_update_slice(
            gathered, piece[None], (place, jnp.int32(0), jnp.int32(0), jnp.int32(0))
        )

    windows = lax.fori_loop(
        0, position_count, cut_one, jnp.zeros((position_count, 2, W, W), jnp.float32)
    )
    win_re = windows[:, 0][:, None]
    win_im = windows[:, 1][:, None]
    probe_re = probe[:, 0][None]
    probe_im = probe[:, 1][None]
    exit_re = probe_re * win_re - probe_im * win_im
    exit_im = probe_re * win_im + probe_im * win_re
    far_re, far_im = transform(exit_re, exit_im, cos_table, sin_table, -1.0)
    amplitude = jnp.sqrt(jnp.sum(far_re * far_re + far_im * far_im, axis=1))
    factor = (1.0 - targets / jnp.maximum(amplitude, amp_floor))[:, None]
    back_re, back_im = transform(far_re * factor, far_im * factor, cos_table, sin_table, 1.0)
    grad_re = jnp.sum(probe_re * back_re + probe_im * back_im, axis=1)
    grad_im = jnp.sum(probe_re * back_im - probe_im * back_re, axis=1)
    probe_grad = jnp.stack(
        [
            jnp.sum(win_re * back_re + win_im * back_im, axis=0),
            jnp.sum(win_re * back_im - win_im * back_re, axis=0),
        ],
        axis=1,
    )
    grad_stack = jnp.stack([grad_re, grad_im], axis=1)

    def add_one(place, accum):
        corner = (jnp.int32(0), row_start[place], col_start[place])
        current = lax.dynamic_slice(accum, corner, (2, W, W))
        return lax.dynamic_update_slice(accum, current + grad_stack[place], corner)

    ext_grad = lax.fori_loop(0, position_count, add_one, jnp.zeros(extended.shape, jnp.float32))
    tile_rows = object_field.shape[1]
    tile_cols = object_field.shape[2]
    padded = extended_2(ext_grad, (("srow", 1), ("scol", 2)), half_width)
    grad_tile = fold_rims(fold_rims(padded, 1, tile_rows, half_width), 2, tile_cols, half_width)
    probe_power = jnp.max(jnp.sum(probe * probe, axis=(0, 1)))
    new_object = object_field - obj_rate * grad_tile / probe_power
    positions_all = PR * row_dev * PC * col_dev
    summed = lax.psum(probe_grad, ("srow", "scol"))
    new_probe = probe - probe_rate * summed / positions_all
    return (new_object, new_probe)


def solution(mesh):
    placed = (P("srow", "scol", None, None), P("srow", "scol", None), P(None, "srow", "scol"), P())
    return jax.shard_map(
        on_device,
        mesh=mesh,
        in_specs=placed,
        out_specs=(P(None, "srow", "scol"), P()),
        check_vma=False,
    )
```

profile of v0, /device:TPU:2, one launch (start us, length us, event | category | flops | bytes accessed | tf_op | source)
XLA Modules:
  0.0 756.6 jit_solution(8100221730847094329)
XLA Ops:
  7.2 2.3 fusion.302
  10.2 1.0 fusion.306
  12.1 2.1 pad_maximum_fusion.10
  14.2 81.5 %all-reduce.3 = (f32[3]{0:T(128)S(1)}, f32[2]{0:T(128)S(1)}) all-reduce(f32[3]{0:T(128)S(1)} %pad_maximum_fusion.10, f32[2]{0:T(128)S(1)} %convolution_bitcast_fusion.4), channel_id=1, replica_groups=mesh['srow'=16,'scol'=16] {'srow','scol'}, use_global_device_ids=true, to_apply=%region_9.10 | all-reduce | flops 5 | bytes 40 | tf_op jit(solution)/shard_map/psum | solution.py:103
  100.3 1.2 collective-permute-start.1
  101.5 73.2 %all-reduce.2 = (f32[2,2]{1,0:T(2,128)S(1)}, f32[2,2]{1,0:T(2,128)S(1)}) all-reduce(f32[2,2]{1,0:T(2,128)S(1)} %convolution_bitcast_fusion.2, f32[2,2]{1,0:T(2,128)S(1)} %convolution_bitcast_fusion.3), channel_id=1, replica_groups=mesh['srow'=16,'scol'=16] {'srow','scol'}, use_global_device_ids=true, to_apply=%region_11.12 | all-reduce | flops 8 | bytes 64 | tf_op jit(solution)/shard_map/psum | solution.py:111
  177.8 1.3 convolution_bitcast_fusion
  179.1 1.3 fusion.49
  183.6 1.2 fusion.103
  184.9 1.2 fusion.101
  186.1 1.2 fusion.50
  187.4 1.2 fusion.51
  188.7 6.0 fusion.95
  194.7 5.8 fusion.99
  200.5 7.0 fusion.45
  207.5 5.8 fusion.46
  213.4 2.9 fusion.97
  217.3 4.1 collective-permute-start.3
  221.8 4.5 collective-permute-done.2
  226.3 3.8 collective-permute-done.3
  230.1 1.2 pad_maximum_fusion.1
  231.2 80.8 %while.26 = (s32[]{:T(128)}, f32[16,2,128,128]{3,2,0,1:T(8,128)S(1)}, s32[16]{0:T(128)S(1)}, s32[16]{0:T(128)S(1)}, f32[2,200,200]{2,1,0:T(8,128)S(1)}, /*index=5*/s32[]{:T(128)}, s32[]{:T(128)}, s32[]{:T(128)}) while((s32[]{:T(128)}, f32[16,2,128,128]{3,2,0,1:T(8,128)S(1)}, s32[16]{0:T(128)S(1)}, s32[16]{0:T(128)S(1)}, ...), condition=%wide.region_1.2_spmd, body=%wide.region_0.1_spmd.sunk | while | flops 8 | bytes 262333 | solution.py:157
  312.0 1.3 slice_bitcast_fusion.1
  313.7 1.6 copy.51
  315.6 2.2 fusion.17
  317.9 2.2 fusion.16
  320.1 2.2 multiply_add_fusion.1
  322.3 3.6 fusion.10
  325.9 3.7 fusion.8
  329.6 2.2 multiply_subtract_fusion.1
  331.8 3.6 multiply_subtract_fusion
  335.4 3.9 add_reduce_fusion.2
  339.3 2.4 fusion.56
  341.7 3.6 fusion.22
  345.3 3.6 fusion.20
  348.9 4.1 fusion.31
  353.0 3.7 fusion.2
  356.6 3.7 fusion
  360.5 3.8 fusion.28
  364.4 3.6 fusion.38
  368.0 5.0 add_reduce_fusion
  373.2 119.0 %while.27 = (s32[]{:T(128)}, f32[2,200,200]{2,1,0:T(8,128)S(1)}, s32[16]{0:T(128)S(1)}, s32[16]{0:T(128)S(1)}, f32[16,2,128,128]{3,2,1,0:T(8,128)S(1)}, /*index=5*/s32[]{:T(128)}, s32[]{:T(128)}, s32[]{:T(128)}) while((s32[]{:T(128)}, f32[2,200,200]{2,1,0:T(8,128)S(1)}, s32[16]{0:T(128)S(1)}, s32[16]{0:T(128)S(1)}, ...), condition=%wide.region_16.17_spmd, body=%wide.region_15.16_spmd.sunk | while | flops 32776 | bytes 655553 | solution.py:186
  378.4 2.3 dynamic_update_slice.18
  385.9 2.3 dynamic_update_slice.18
  393.4 2.3 dynamic_update_slice.18
  401.0 2.3 dynamic_update_slice.18
  408.5 2.3 dynamic_update_slice.18
  416.0 2.3 dynamic_update_slice.18
  423.5 2.2 dynamic_update_slice.18
  430.9 2.2 dynamic_update_slice.18
  438.3 2.2 dynamic_update_slice.18
  445.8 2.2 dynamic_update_slice.18
  453.2 2.2 dynamic_update_slice.18
  460.6 2.2 dynamic_update_slice.18
  468.0 2.2 dynamic_update_slice.18
  475.4 2.2 dynamic_update_slice.18
  482.8 2.1 dynamic_update_slice.18
  490.1 2.1 dynamic_update_slice.18
  493.1 4.2 collective-permute-start.5
  497.3 1.8 collective-permute-done.4
  500.1 4.1 collective-permute-start.7
  504.2 241.1 %all-reduce.6.cloned.1.call-done = f32[2,2,128,128]{3,2,1,0:T(8,128)} async-done(((f32[2,2,128,128]{3,2,1,0:T(8,128)}), f32[2,2,128,128]{3,2,1,0:T(8,128)}) %all-reduce.6.cloned.1.call-update) | async-done | bytes 262160 | tf_op jit(solution)/shard_map/psum | solution.py:194
  745.4 1.7 multiply_subtract_fusion.10
  748.2 1.4 fusion.85
  (179 shorter events, 53.6 us)
Async XLA Ops:
  7.2 170.6 %copy-start = (f32[4,4,128,128]{3,2,1,0:T(8,128)S(1)}, f32[4,4,128,128]{3,2,1,0:T(8,128)}, u32[]{:S(2)}) copy-start(f32[4,4,128,128]{3,2,1,0:T(8,128)} %param.8) | copy-start | bytes 3145732
  7.2 738.2 %all-reduce.6.cloned.1.call-start = ((), (), s32[]{:S(2)}) async-start(), calls=%async_computation | async-start | bytes 524288 | tf_op jit(solution)/shard_map/psum | solution.py:194
  14.1 202.9 %collective-permute-start = (f32[2,64,72]{2,1,0:T(8,128)S(1)}, f32[2,64,72]{2,1,0:T(8,128)S(1)}, u32[]{:S(2)}, u32[]{:S(2)}) collective-permute-start(f32[2,64,72]{2,1,0:T(8,128)S(1)} %get-tuple-element.249), channel_id=1, source_target_pairs={{0,16},{16,32},{32,48},{48,64},{64,80},{80,96},{96,112},{112,128},... | collective-permute-start | bytes 110600 | tf_op jit(solution)/shard_map/ppermute | solution.py:23
  100.3 116.8 %collective-permute-start.1 = (f32[2,64,72]{2,1,0:T(8,128)S(1)}, f32[2,64,72]{2,1,0:T(8,128)S(1)}, u32[]{:S(2)}, u32[]{:S(2)}) collective-permute-start(f32[2,64,72]{2,1,0:T(8,128)S(1)} %get-tuple-element.248), channel_id=1, source_target_pairs={{16,0},{32,16},{48,32},{64,48},{80,64},{96,80},{112,96},{128,112},... | collective-permute-start | bytes 110600 | tf_op jit(solution)/shard_map/ppermute | solution.py:25
  213.3 3.0 copy-start.3
  213.3 3.7 copy-start.5
  213.3 8.1 %copy-start.10 = (s32[4,4,2]{1,2,0:T(2,128)S(1)}, s32[4,4,2]{1,2,0:T(2,128)}, u32[]{:S(2)}) copy-start(s32[4,4,2]{1,2,0:T(2,128)} %param.9) | copy-start | bytes 388
  217.2 9.1 %collective-permute-start.2 = (f32[2,200,64]{2,1,0:T(8,128)S(1)}, f32[2,200,64]{2,1,0:T(8,128)S(1)}, u32[]{:S(2)}, u32[]{:S(2)}) collective-permute-start(f32[2,200,64]{2,1,0:T(8,128)S(1)} %get-tuple-element.246), channel_id=1, source_target_pairs={{0,1},{1,2},{2,3},{3,4},{4,5},{5,6},{6,7},{7,8},{8,9},{9,10},{10,1... | collective-permute-start | bytes 307208 | tf_op jit(solution)/shard_map/ppermute | solution.py:23
  217.3 12.8 %collective-permute-start.3 = (f32[2,200,64]{2,1,0:T(8,128)S(1)}, f32[2,200,64]{2,1,0:T(8,128)}, u32[]{:S(2)}, u32[]{:S(2)}) collective-permute-start(f32[2,200,64]{2,1,0:T(8,128)S(1)} %get-tuple-element.247), channel_id=1, source_target_pairs={{1,0},{2,1},{3,2},{4,3},{5,4},{6,5},{7,6},{8,7},{9,8},{10,9},{11,1... | collective-permute-start | bytes 307208 | tf_op jit(solution)/shard_map/ppermute | solution.py:25
  312.0 1.7 copy-start.1
  335.4 3.9 copy-start.6
  335.4 3.9 copy-start.7
  356.6 3.7 copy-start.2
  364.4 3.6 copy-start.8
  364.4 3.6 copy-start.9
  492.2 253.1 %copy-start.4 = (f32[2,2,128,128]{3,2,1,0:T(8,128)S(1)}, f32[2,2,128,128]{3,2,1,0:T(8,128)}, u32[]{:S(2)}) copy-start(f32[2,2,128,128]{3,2,1,0:T(8,128)} %param.11) | copy-start | bytes 786436
  492.3 6.9 collective-permute-start.4
  492.4 255.4 %copy-start.11 = (pred[72]{0:T(512)(128)(4,1)S(1)}, pred[72]{0:T(512)(128)(4,1)}, u32[]{:S(2)}) copy-start(pred[72]{0:T(512)(128)(4,1)} %constant.140.clone.1) | copy-start | bytes 220
  493.1 6.7 collective-permute-start.5
  500.0 247.8 %collective-permute-start.6 = (f32[2,328,64]{2,1,0:T(8,128)S(1)}, f32[2,328,64]{2,1,0:T(8,128)S(1)}, u32[]{:S(2)}, u32[]{:S(2)}) collective-permute-start(f32[2,328,64]{2,1,0:T(8,128)S(1)} %get-tuple-element.236), channel_id=1, source_target_pairs={{0,1},{1,2},{2,3},{3,4},{4,5},{5,6},{6,7},{7,8},{8,9},{9,10},{10,1... | collective-permute-start | bytes 503816 | tf_op jit(solution)/shard_map/ppermute | solution.py:23
  500.1 247.7 %collective-permute-start.7 = (f32[2,328,64]{2,1,0:T(8,128)S(1)}, f32[2,328,64]{2,1,0:T(8,128)S(1)}, u32[]{:S(2)}, u32[]{:S(2)}) collective-permute-start(f32[2,328,64]{2,1,0:T(8,128)S(1)} %get-tuple-element.237), channel_id=1, source_target_pairs={{1,0},{2,1},{3,2},{4,3},{5,4},{6,5},{7,6},{8,7},{9,8},{10,9},{11,1... | collective-permute-start | bytes 503816 | tf_op jit(solution)/shard_map/ppermute | solution.py:25
Sparse Core Ops, SparseCore 0:
  493.2 252.0 all-reduce.5
where the time goes:
time: 763 us; the launch traced here: 757 us
  waiting for transfers between devices  252 us (33%)
  blocking collectives  155 us (20%)
  loops' own time  122 us (16%)
  matrix products  93.4 us (12%)
  local copies, waits for them, and re-layouts  83.1 us (11%)
  between operations  21.2 us (3%)
  other arithmetic  16.3 us (2%)
  starting transfers between devices  14 us (2%)
    psum x1, waiting for transfers between devices, on_device(): summed = lax.psum(probe_grad, ('srow', 'scol'))  241 us
    psum x1, blocking collectives, on_device(): lax.psum((first_sums, centre_moment), ('srow', 'scol'))  81.5 us
    psum x1, blocking collectives, on_device(): second_mom, cross_mom = lax.psum((second_mom, cross_mom), ('srow', 'scol'))  73.2 us
    another operation x1, loops' own time, on_device(): lax.fori_loop(0, position_count, add_one, jnp.zeros(extended.shape, jnp.f...  62.7 us
    another operation x1, loops' own time, on_device(): lax.fori_loop(0, position_count, cut_one, jnp.zeros((position_count, 2, W...  59.2 us
    dot_general x14, matrix products, rows_by(): return jnp.einsum('uk,...kv->...uv', matrix, values, precision=highest)  51.1 us
    dot_general x14, matrix products, cols_by(): return jnp.einsum('...uk,kv->...uv', values, matrix, precision=highest)  40.9 us
    dynamic_update_slice x16, local copies, waits for them, and re-layouts, add_one(): return lax.dynamic_update_slice(accum, current + grad_stack[place], corner)  35.7 us
  transfers between devices with their start and end apart: 9, of which 5 were waited for; matrix products, arithmetic and copies ran while one was open for 6% of the time, Pallas kernels for 0%

commit v1 on v0

--- a/solution.py
+++ b/solution.py
@@ -191,7 +191,9 @@
     probe_power = jnp.max(jnp.sum(probe * probe, axis=(0, 1)))
     new_object = object_field - obj_rate * grad_tile / probe_power
     positions_all = PR * row_dev * PC * col_dev
-    summed = lax.psum(probe_grad, ("srow", "scol"))
+    summed = probe_grad
+    for mesh_axis in ("srow", "scol"):
+        summed = lax.psum(summed, mesh_axis)
     new_probe = probe - probe_rate * summed / positions_all
     return (new_object, new_probe)
 

time: 763 us -> 793 us (1.039)
  waiting for transfers between devices: 252 us -> 282 us
    psum x1 -> x2, waiting for transfers between devices: 241 us -> 271 us  [on_device(): summed = lax.psum(summed, mesh_axis)]
  transfers between devices with their start and end apart: 9 -> 10, of which waited for: 5 -> 6; matrix products, arithmetic and copies ran while one was open for 6% -> 5% of each run, Pallas kernels for 0% -> 0%
where the time goes in v1:
time: 793 us; the launch traced here: 787 us
  waiting for transfers between devices  282 us (36%)
  blocking collectives  155 us (20%)
  loops' own time  122 us (15%)
  matrix products  94 us (12%)
  local copies, waits for them, and re-layouts  82.9 us (10%)
  between operations  21.3 us (3%)
  other arithmetic  16.3 us (2%)
  starting transfers between devices  14 us (2%)
    psum x2, waiting for transfers between devices, on_device(): summed = lax.psum(summed, mesh_axis)  271 us
    psum x1, blocking collectives, on_device(): lax.psum((first_sums, centre_moment), ('srow', 'scol'))  81.5 us
    psum x1, blocking collectives, on_device(): second_mom, cross_mom = lax.psum((second_mom, cross_mom), ('srow', 'scol'))  73.3 us
    another operation x1, loops' own time, on_device(): lax.fori_loop(0, position_count, add_one, jnp.zeros(extended.shape, jnp.f...  62.7 us
    another operation x1, loops' own time, on_device(): lax.fori_loop(0, position_count, cut_one, jnp.zeros((position_count, 2, W...  59.2 us
    dot_general x14, matrix products, rows_by(): return jnp.einsum('uk,...kv->...uv', matrix, values, precision=highest)  51.4 us
    dot_general x14, matrix products, cols_by(): return jnp.einsum('...uk,kv->...uv', values, matrix, precision=highest)  41.1 us
    dynamic_update_slice x16, local copies, waits for them, and re-layouts, add_one(): return lax.dynamic_update_slice(accum, current + grad_stack[place], corner)  35.5 us
  transfers between devices with their start and end apart: 10, of which 6 were waited for; matrix products, arithmetic and copies ran while one was open for 5% of the time, Pallas kernels for 0%

profile of v1, /device:TPU:2, one launch (start us, length us, event | category | flops | bytes accessed | tf_op | source)
XLA Modules:
  0.0 787.3 jit_solution(7100399150542651007)
XLA Ops:
  7.2 2.3 fusion.302
  12.1 2.1 pad_maximum_fusion.10
  14.2 81.5 %all-reduce.3 = (f32[3]{0:T(128)S(1)}, f32[2]{0:T(128)S(1)}) all-reduce(f32[3]{0:T(128)S(1)} %pad_maximum_fusion.10, f32[2]{0:T(128)S(1)} %convolution_bitcast_fusion.4), channel_id=1, replica_groups=mesh['srow'=16,'scol'=16] {'srow','scol'}, use_global_device_ids=true, to_apply=%region_9.10 | all-reduce | flops 5 | bytes 40 | tf_op jit(solution)/shard_map/psum | solution.py:103
  100.3 1.2 collective-permute-start.1
  101.5 73.3 %all-reduce.2 = (f32[2,2]{1,0:T(2,128)S(1)}, f32[2,2]{1,0:T(2,128)S(1)}) all-reduce(f32[2,2]{1,0:T(2,128)S(1)} %convolution_bitcast_fusion.2, f32[2,2]{1,0:T(2,128)S(1)} %convolution_bitcast_fusion.3), channel_id=1, replica_groups=mesh['srow'=16,'scol'=16] {'srow','scol'}, use_global_device_ids=true, to_apply=%region_11.12 | all-reduce | flops 8 | bytes 64 | tf_op jit(solution)/shard_map/psum | solution.py:111
  177.8 1.3 convolution_bitcast_fusion
  179.1 1.3 fusion.49
  183.6 1.2 fusion.103
  184.9 1.2 fusion.101
  186.1 1.2 fusion.50
  187.3 1.2 fusion.51
  188.6 6.0 fusion.95
  194.6 5.8 fusion.99
  200.4 7.0 fusion.45
  207.4 5.8 fusion.46
  213.2 2.9 fusion.97
  217.2 4.1 collective-permute-start.3
  221.7 4.5 collective-permute-done.2
  226.2 3.8 collective-permute-done.3
  229.9 1.2 pad_maximum_fusion.1
  231.1 80.8 %while.26 = (s32[]{:T(128)}, f32[16,2,128,128]{3,2,0,1:T(8,128)S(1)}, s32[16]{0:T(128)S(1)}, s32[16]{0:T(128)S(1)}, f32[2,200,200]{2,1,0:T(8,128)S(1)}, /*index=5*/s32[]{:T(128)}, s32[]{:T(128)}, s32[]{:T(128)}) while((s32[]{:T(128)}, f32[16,2,128,128]{3,2,0,1:T(8,128)S(1)}, s32[16]{0:T(128)S(1)}, s32[16]{0:T(128)S(1)}, ...), condition=%wide.region_1.2_spmd, body=%wide.region_0.1_spmd.sunk | while | flops 8 | bytes 262333 | solution.py:157
  311.9 1.3 slice_bitcast_fusion.1
  313.6 1.6 copy.51
  315.5 2.2 fusion.17
  317.7 2.2 fusion.16
  320.0 2.3 multiply_add_fusion.1
  322.3 3.6 fusion.10
  325.9 3.8 fusion.8
  329.6 2.3 multiply_subtract_fusion.1
  331.9 3.6 multiply_subtract_fusion
  335.5 4.0 add_reduce_fusion.2
  339.6 2.4 fusion.56
  342.0 3.6 fusion.22
  345.6 3.6 fusion.20
  349.3 4.1 fusion.31
  353.4 3.7 fusion.2
  357.1 3.6 fusion
  360.9 3.9 fusion.28
  364.8 3.6 fusion.38
  368.5 5.1 add_reduce_fusion
  373.8 118.8 %while.27 = (s32[]{:T(128)}, f32[2,200,200]{2,1,0:T(8,128)S(1)}, s32[16]{0:T(128)S(1)}, s32[16]{0:T(128)S(1)}, f32[16,2,128,128]{3,2,1,0:T(8,128)S(1)}, /*index=5*/s32[]{:T(128)}, s32[]{:T(128)}, s32[]{:T(128)}) while((s32[]{:T(128)}, f32[2,200,200]{2,1,0:T(8,128)S(1)}, s32[16]{0:T(128)S(1)}, s32[16]{0:T(128)S(1)}, ...), condition=%wide.region_16.17_spmd, body=%wide.region_15.16_spmd.sunk | while | flops 32776 | bytes 655553 | solution.py:186
  379.0 2.3 dynamic_update_slice.18
  386.5 2.3 dynamic_update_slice.18
  394.1 2.3 dynamic_update_slice.18
  401.6 2.3 dynamic_update_slice.18
  409.1 2.2 dynamic_update_slice.18
  416.5 2.3 dynamic_update_slice.18
  424.0 2.2 dynamic_update_slice.18
  431.4 2.2 dynamic_update_slice.18
  438.9 2.2 dynamic_update_slice.18
  446.3 2.2 dynamic_update_slice.18
  453.7 2.2 dynamic_update_slice.18
  461.1 2.2 dynamic_update_slice.18
  468.5 2.1 dynamic_update_slice.18
  475.8 2.2 dynamic_update_slice.18
  483.2 2.1 dynamic_update_slice.18
  490.5 2.1 dynamic_update_slice.18
  493.6 4.2 collective-permute-start.5
  497.8 1.8 collective-permute-done.4
  500.6 4.1 collective-permute-start.7
  504.7 125.4 %all-reduce.7.cloned.1.call-done = f32[2,2,128,128]{3,2,1,0:T(8,128)} async-done(((f32[2,2,128,128]{3,2,1,0:T(8,128)}), f32[2,2,128,128]{3,2,1,0:T(8,128)}) %all-reduce.7.cloned.1.call-update) | async-done | bytes 262160 | tf_op jit(solution)/shard_map/psum | solution.py:196
  630.5 145.9 %all-reduce.9.cloned.1.call-done = f32[2,2,128,128]{3,2,1,0:T(8,128)} async-done(((f32[2,2,128,128]{3,2,1,0:T(8,128)}), f32[2,2,128,128]{3,2,1,0:T(8,128)}) %all-reduce.9.cloned.1.call-update) | async-done | bytes 262160 | tf_op jit(solution)/shard_map/psum | solution.py:196
  776.4 1.7 multiply_subtract_fusion.10
  778.8 1.4 fusion.85
  (182 shorter events, 54.7 us)
Async XLA Ops:
  7.2 170.6 %copy-start = (f32[4,4,128,128]{3,2,1,0:T(8,128)S(1)}, f32[4,4,128,128]{3,2,1,0:T(8,128)}, u32[]{:S(2)}) copy-start(f32[4,4,128,128]{3,2,1,0:T(8,128)} %param.8) | copy-start | bytes 3145732
  7.2 622.9 %all-reduce.7.cloned.1.call-start = ((), (), s32[]{:S(2)}) async-start(), calls=%async_computation | async-start | bytes 524288 | tf_op jit(solution)/shard_map/psum | solution.py:196
  14.1 202.7 %collective-permute-start = (f32[2,64,72]{2,1,0:T(8,128)S(1)}, f32[2,64,72]{2,1,0:T(8,128)S(1)}, u32[]{:S(2)}, u32[]{:S(2)}) collective-permute-start(f32[2,64,72]{2,1,0:T(8,128)S(1)} %get-tuple-element.249), channel_id=1, source_target_pairs={{0,16},{16,32},{32,48},{48,64},{64,80},{80,96},{96,112},{112,128},... | collective-permute-start | bytes 110600 | tf_op jit(solution)/shard_map/ppermute | solution.py:23
  100.3 116.7 %collective-permute-start.1 = (f32[2,64,72]{2,1,0:T(8,128)S(1)}, f32[2,64,72]{2,1,0:T(8,128)S(1)}, u32[]{:S(2)}, u32[]{:S(2)}) collective-permute-start(f32[2,64,72]{2,1,0:T(8,128)S(1)} %get-tuple-element.248), channel_id=1, source_target_pairs={{16,0},{32,16},{48,32},{64,48},{80,64},{96,80},{112,96},{128,112},... | collective-permute-start | bytes 110600 | tf_op jit(solution)/shard_map/ppermute | solution.py:25
  213.2 3.0 copy-start.3
  213.2 3.7 copy-start.5
  213.2 8.1 %copy-start.10 = (s32[4,4,2]{1,2,0:T(2,128)S(1)}, s32[4,4,2]{1,2,0:T(2,128)}, u32[]{:S(2)}) copy-start(s32[4,4,2]{1,2,0:T(2,128)} %param.9) | copy-start | bytes 388
  217.1 9.1 %collective-permute-start.2 = (f32[2,200,64]{2,1,0:T(8,128)S(1)}, f32[2,200,64]{2,1,0:T(8,128)S(1)}, u32[]{:S(2)}, u32[]{:S(2)}) collective-permute-start(f32[2,200,64]{2,1,0:T(8,128)S(1)} %get-tuple-element.246), channel_id=1, source_target_pairs={{0,1},{1,2},{2,3},{3,4},{4,5},{5,6},{6,7},{7,8},{8,9},{9,10},{10,1... | collective-permute-start | bytes 307208 | tf_op jit(solution)/shard_map/ppermute | solution.py:23
  217.2 12.8 %collective-permute-start.3 = (f32[2,200,64]{2,1,0:T(8,128)S(1)}, f32[2,200,64]{2,1,0:T(8,128)}, u32[]{:S(2)}, u32[]{:S(2)}) collective-permute-start(f32[2,200,64]{2,1,0:T(8,128)S(1)} %get-tuple-element.247), channel_id=1, source_target_pairs={{1,0},{2,1},{3,2},{4,3},{5,4},{6,5},{7,6},{8,7},{9,8},{10,9},{11,1... | collective-permute-start | bytes 307208 | tf_op jit(solution)/shard_map/ppermute | solution.py:25
  311.9 1.7 copy-start.1
  335.5 4.0 copy-start.6
  335.5 4.0 copy-start.7
  357.1 3.6 copy-start.2
  364.8 3.6 copy-start.8
  364.8 3.6 copy-start.9
  492.7 137.5 %copy-start.11 = (pred[72]{0:T(512)(128)(4,1)S(1)}, pred[72]{0:T(512)(128)(4,1)}, u32[]{:S(2)}) copy-start(pred[72]{0:T(512)(128)(4,1)} %constant.140.clone.1) | copy-start | bytes 220
  492.7 6.9 collective-permute-start.4
  493.5 282.9 %all-reduce.9.cloned.1.call-start = ((), (), s32[]{:S(2)}) async-start(), calls=%async_computation.1 | async-start | bytes 524288 | tf_op jit(solution)/shard_map/psum | solution.py:196
  493.6 6.7 collective-permute-start.5
  499.6 276.8 %copy-start.4 = (f32[2,2,128,128]{3,2,1,0:T(8,128)S(1)}, f32[2,2,128,128]{3,2,1,0:T(8,128)}, u32[]{:S(2)}) copy-start(f32[2,2,128,128]{3,2,1,0:T(8,128)} %param.11) | copy-start | bytes 786436
  500.5 129.6 %collective-permute-start.6 = (f32[2,328,64]{2,1,0:T(8,128)S(1)}, f32[2,328,64]{2,1,0:T(8,128)S(1)}, u32[]{:S(2)}, u32[]{:S(2)}) collective-permute-start(f32[2,328,64]{2,1,0:T(8,128)S(1)} %get-tuple-element.236), channel_id=1, source_target_pairs={{0,1},{1,2},{2,3},{3,4},{4,5},{5,6},{6,7},{7,8},{8,9},{9,10},{10,1... | collective-permute-start | bytes 503816 | tf_op jit(solution)/shard_map/ppermute | solution.py:23
  500.6 129.6 %collective-permute-start.7 = (f32[2,328,64]{2,1,0:T(8,128)S(1)}, f32[2,328,64]{2,1,0:T(8,128)S(1)}, u32[]{:S(2)}, u32[]{:S(2)}) collective-permute-start(f32[2,328,64]{2,1,0:T(8,128)S(1)} %get-tuple-element.237), channel_id=1, source_target_pairs={{1,0},{2,1},{3,2},{4,3},{5,4},{6,5},{7,6},{8,7},{9,8},{10,9},{11,1... | collective-permute-start | bytes 503816 | tf_op jit(solution)/shard_map/ppermute | solution.py:25
Sparse Core Ops, SparseCore 0:
  493.6 136.3 all-reduce.6
  632.9 143.5 all-reduce.8
